TPU v7x, 256 devices: a whole 4x4x8 slice. The times are simulated.
256 devices in a mesh: sub: 16 (over z, core), row: 16 (over y, x).
Axes of the slice: x: 4, y: 4, z: 8, core: 2. Of those that a mesh axis runs over, the one named last changes fastest.
Arguments:
- modes: float32 [196608, 64], P(('sub', 'row')), may hold values from -6 to 6
- search: float32 [196608, 64], P(('sub', 'row')), may hold values from -6 to 6
- precond: float32 [196608], P(('sub', 'row')), may hold values from 0.05 to 0.25
- in_row: int32 [16, 16, 96], P('sub', 'row'), may hold values from 0 to 11, as said below
- in_col: int32 [16, 16, 96], P('sub', 'row'), may hold values from 0 to 191, as said below
- in_val: bfloat16 [16, 16, 96, 64, 64], P('sub', 'row'), as said below
- bnd_rows: int32 [16, 16, 3], P('sub', 'row'), may hold values from 0 to 11, as said below
- if_row: int32 [16, 16, 12], P('sub', 'row'), may hold values from 0 to 11, as said below
- if_src: int32 [16, 16, 12], P('sub', 'row'), may hold values from 0 to 47, as said below
- if_val: bfloat16 [16, 16, 12, 64, 64], P('sub', 'row')
Outputs:
- modes_out: float32 [196608, 64], P(('sub', 'row'))
- search_out: float32 [196608, 64], P(('sub', 'row'))
Inputs may be any that keep to these rules, and one draw needn't show every extreme that they name: `in_row`: entry k < 12 is k; each later group of 12 entries names each of the device's block-rows once. `in_col`: entry k < 12 is r * 12 + k on device (s, r); in each later group of 12 entries the devices of a subdomain together name each of its 192 block-rows once, and no entry names its own block-row. `in_val`: the first 12 blocks of every device are symmetric; the operator A is symmetric positive definite. `bnd_rows`: distinct within a device. `if_row`: each of the device's 12 block-rows once. `if_src`: t * 3 + q with t never the device's own subdomain; among the devices with one index of row, each boundary slot of each subdomain is named exactly 4 times.
All inputs are finite; a program needn't handle non-finite values.
Results may differ from a plain program's by a relative error of at most 0.0006.
Values may be sent and summed in bfloat16 or wider, within the bound.
A program may use at most 128 MiB of HBM per device.

v0:
```python
import jax
import jax.numpy as jnp
from jax import lax
from jax.sharding import PartitionSpec as P

KB = 64
LB = 12
ITERS = 2
IFR = 3
precise_mode = lax.Precision.HIGHEST


def gram_product(left, right):
    return jnp.dot(left.T, right, precision=precise_mode, preferred_element_type=jnp.float32)


def full_dot(left, right):
    return jnp.dot(left, right, precision=precise_mode, preferred_element_type=jnp.float32)


def chol_solve(matrix, rhs):
    factor = jnp.linalg.cholesky(matrix)
    halfway = lax.linalg.triangular_solve(factor, rhs, left_side=True, lower=True)
    return lax.linalg.triangular_solve(
        factor, halfway, left_side=True, lower=True, transpose_a=True
    )


def rescale(factor, moved):
    return lax.linalg.triangular_solve(factor, moved, left_side=False, lower=True, transpose_a=True)


def project(current, image_x):
    return lax.psum(
        (gram_product(current, current), gram_product(current, image_x)), ("sub", "row")
    )


def apply_blocks(vector, blocks):
    rows_here, cols_here, vals_here, bnd_here, face_rows, face_src, face_vals = blocks
    width = vector.shape[1]
    mine = vector.reshape(LB, KB, width)
    local_ids = jnp.arange(LB, dtype=jnp.int32)
    position = lax.axis_index("row")
    group = lax.all_gather(vector, "row", axis=0, tiled=True).reshape(-1, KB, width)
    forward = jnp.einsum("kij,kjw->kiw", vals_here, group[cols_here], precision=precise_mode)
    select = (rows_here[:, None] == local_ids[None, :]).astype(jnp.float32)
    result = jnp.einsum("ka,kiw->aiw", select, forward, precision=precise_mode)
    backward = jnp.einsum("kji,kjw->kiw", vals_here, mine[rows_here], precision=precise_mode)
    keeper = (cols_here != position * LB + rows_here).astype(jnp.float32)
    backward = backward * keeper[:, None, None]
    wanted = jnp.arange(LB * KB * lax.axis_size("row") // KB, dtype=jnp.int32)
    chosen = (cols_here[None, :] == wanted[:, None]).astype(jnp.float32)
    returned = lax.psum_scatter(
        jnp.einsum("bk,kiw->biw", chosen, backward, precision=precise_mode).reshape(
            LB * KB * lax.axis_size("row"), width
        ),
        "row",
        scatter_dimension=0,
        tiled=True,
    )
    result = result + returned.reshape(LB, KB, width)
    boundary = mine[bnd_here].reshape(-1, width)
    remote = lax.all_gather(boundary, "sub", axis=0, tiled=True).reshape(-1, KB, width)
    forward = jnp.einsum("kij,kjw->kiw", face_vals, remote[face_src], precision=precise_mode)
    face_select = (face_rows[:, None] == local_ids[None, :]).astype(jnp.float32)
    result = result + jnp.einsum("ka,kiw->aiw", face_select, forward, precision=precise_mode)
    backward = jnp.einsum("kji,kjw->kiw", face_vals, mine[face_rows], precision=precise_mode)
    wanted = jnp.arange(IFR * KB * lax.axis_size("sub") // KB, dtype=jnp.int32)
    chosen = (face_src[None, :] == wanted[:, None]).astype(jnp.float32)
    landed = lax.psum_scatter(
        jnp.einsum("bk,kiw->biw", chosen, backward, precision=precise_mode).reshape(
            IFR * KB * lax.axis_size("sub"), width
        ),
        "sub",
        scatter_dimension=0,
        tiled=True,
    ).reshape(IFR, KB, width)
    placed = (bnd_here[:, None] == local_ids[None, :]).astype(jnp.float32)
    result = result + jnp.einsum("qa,qiw->aiw", placed, landed, precision=precise_mode)
    return result.reshape(LB * KB, width)


def local(modes, search, precond, in_row, in_col, in_val, bnd_rows, if_row, if_src, if_val):
    blocks = (
        in_row[0, 0],
        in_col[0, 0],
        in_val[0, 0].astype(jnp.float32),
        bnd_rows[0, 0],
        if_row[0, 0],
        if_src[0, 0],
        if_val[0, 0].astype(jnp.float32),
    )
    total_rows = modes.shape[0] * lax.axis_size("sub") * lax.axis_size("row")
    nmode = modes.shape[1]
    images = apply_blocks(jnp.concatenate([modes, search], 1), blocks)
    current, direction = (modes, search)
    image_x, image_p = (images[:, :nmode], images[:, nmode:])
    for sweep in range(ITERS):
        correlation, energy = project(current, image_x)
        ritz = chol_solve(correlation, energy)
        residue = image_x - full_dot(current, ritz)
        update = precond[:, None] * residue
        image_w = apply_blocks(update, blocks)
        basis = jnp.concatenate([update, direction], 1)
        image_b = jnp.concatenate([image_w, image_p], 1)
        coupled, driving = lax.psum(
            (gram_product(basis, image_b), gram_product(basis, image_x)), ("sub", "row")
        )
        coeffs = -chol_solve(coupled, driving)
        step_x = full_dot(basis, coeffs)
        step_a = full_dot(image_b, coeffs)
        moved = current + step_x
        moved_image = image_x + step_a
        lengths = lax.psum(gram_product(moved, moved), ("sub", "row"))
        factor = jnp.linalg.cholesky(lengths / total_rows)
        current = rescale(factor, moved)
        image_x = rescale(factor, moved_image)
        direction = rescale(factor, step_x)
        image_p = rescale(factor, step_a)
    return (current, direction)


def solution(mesh):
    return jax.shard_map(
        local,
        mesh=mesh,
        in_specs=(
            P(("sub", "row"), None),
            P(("sub", "row"), None),
            P(("sub", "row")),
            P("sub", "row", None),
            P("sub", "row", None),
            P("sub", "row", None, None, None),
            P("sub", "row", None),
            P("sub", "row", None),
            P("sub", "row", None),
            P("sub", "row", None, None, None),
        ),
        out_specs=(P(("sub", "row"), None), P(("sub", "row"), None)),
        check_vma=False,
    )
```

profile of v0, /device:TPU:1, one launch (start us, length us, event | category | flops | bytes accessed | tf_op | source)
XLA Modules:
  0.0 1590.2 jit_solution(9537704448237477838)
XLA Ops:
  19.7 2.8 copy.144
  22.5 3.7 multiply_bitcast_fusion.2
  26.3 4.6 fusion
  30.9 6.3 copy.146
  37.5 3.3 copy.142
  41.8 13.2 all-gather.9.cloned.1.call-done
  57.4 53.8 %reduce-scatter.13.cloned.1.call-done = f32[192,128]{1,0:T(8,128)} async-done(((f32[3072,128]{1,0:T(8,128)}), f32[192,128]{1,0:T(8,128)}) %reduce-scatter.13.cloned.1.call-update) | async-done | bytes 98320 | tf_op jit(solution)/shard_map/reduce_scatter | solution.py:71
  112.6 69.1 %all-gather.7.cloned.1.call-done = f32[12288,128]{1,0:T(8,128)} async-done(((f32[768,128]{1,0:T(8,128)}), f32[12288,128]{1,0:T(8,128)}) %all-gather.7.cloned.1.call-update) | async-done | bytes 6291472 | tf_op jit(solution)/shard_map/all_gather | solution.py:45
  181.7 5.2 gather_fusion
  186.9 5.3 convolution_bitcast_fusion.2
  192.2 78.6 %reduce-scatter.11.cloned.1.call-done = f32[768,128]{1,0:T(8,128)} async-done(((f32[12288,128]{1,0:T(8,128)}), f32[768,128]{1,0:T(8,128)}) %reduce-scatter.11.cloned.1.call-update) | async-done | bytes 393232 | tf_op jit(solution)/shard_map/reduce_scatter | solution.py:54
  270.8 4.8 fusion.7
  277.3 76.9 %all-reduce.1 = (f32[64,64]{0,1:T(8,128)S(1)}, f32[64,64]{0,1:T(8,128)S(1)}) all-reduce(f32[64,64]{0,1:T(8,128)S(1)} %convolution_bitcast_fusion.16, f32[64,64]{0,1:T(8,128)} %fusion.130), channel_id=1, replica_groups=mesh['sub'=16,'row'=16] {'sub','row'}, use_global_device_ids=true, to_apply=%region_5.0 | all-reduce | flops 8192 | bytes 65536 | tf_op jit(solution)/shard_map/psum | solution.py:34
  354.3 5.8 cholesky.116
  361.5 4.9 custom-call.29
  371.9 2.7 fusion.15
  374.6 3.1 copy.246
  378.6 2.6 gather_fusion.6
  381.2 6.5 multiply_bitcast_fusion.1
  387.7 4.7 copy.164
  392.4 5.5 fusion.44
  397.9 6.3 copy.165
  404.2 5.9 reshape.293
  411.0 21.9 %all-gather = f32[16,192,64]{1,2,0:T(8,128)} all-gather(f32[1,192,64]{1,2,0:T(8,128)S(1)} %copy.168), channel_id=1, replica_groups=mesh['sub'=16,'row'=16] {'sub'}, dimensions={0}, use_global_device_ids=true | all-gather | bytes 835584 | tf_op jit(solution)/shard_map/all_gather | solution.py:64
  432.9 2.9 copy.234
  441.7 45.4 %all-gather.11.cloned.1.call-done = f32[12288,64]{0,1:T(8,128)} async-done(((f32[768,64]{0,1:T(8,128)}), f32[12288,64]{0,1:T(8,128)}) %all-gather.11.cloned.1.call-update) | async-done | bytes 3145744 | tf_op jit(solution)/shard_map/all_gather | solution.py:45
  487.1 5.8 copy.233
  492.8 5.3 gather_fusion.5
  498.1 6.2 convolution_bitcast_fusion.1
  504.4 4.7 copy.160
  509.1 60.1 %reduce-scatter.15.cloned.1.call-done = f32[768,64]{0,1:T(8,128)} async-done(((f32[12288,64]{0,1:T(8,128)}), f32[768,64]{0,1:T(8,128)}) %reduce-scatter.15.cloned.1.call-update) | async-done | bytes 196624 | tf_op jit(solution)/shard_map/reduce_scatter | solution.py:54
  573.2 4.3 convolution_add_fusion.4
  582.2 77.9 %psum.73 = f32[128,64]{0,1:T(8,128)S(1)} all-reduce(f32[128,64]{0,1:T(8,128)} %fusion.27), channel_id=1, replica_groups=mesh['sub'=16,'row'=16] {'sub','row'}, use_global_device_ids=true, to_apply=%region_11.16 | all-reduce | flops 8192 | bytes 65536 | tf_op jit(solution)/shard_map/psum | solution.py:107
  660.1 160.0 %all-reduce.5.cloned.1.call-done = f32[128,128]{0,1:T(8,128)} async-done(((f32[128,128]{0,1:T(8,128)}), f32[128,128]{0,1:T(8,128)}) %all-reduce.5.cloned.1.call-update) | async-done | bytes 65552 | tf_op jit(solution)/shard_map/psum | solution.py:107
  821.9 11.7 cholesky.127
  835.0 9.8 custom-call.31
  847.9 74.6 %psum.74 = f32[64,64]{0,1:T(8,128)S(1)} all-reduce(f32[64,64]{0,1:T(8,128)S(1)} %fusion.131), channel_id=1, replica_groups=mesh['sub'=16,'row'=16] {'sub','row'}, use_global_device_ids=true, to_apply=%region_12.19 | all-reduce | flops 4096 | bytes 32768 | tf_op jit(solution)/shard_map/psum | solution.py:115
  922.5 5.8 cholesky.138
  929.7 4.9 custom-call.32
  937.0 74.2 %all-reduce = (f32[64,64]{1,0:T(8,128)S(1)}, f32[64,64]{0,1:T(8,128)S(1)}) all-reduce(f32[64,64]{1,0:T(8,128)S(1)} %fusion.133, f32[64,64]{0,1:T(8,128)S(1)} %fusion.132), channel_id=1, replica_groups=mesh['sub'=16,'row'=16] {'sub','row'}, use_global_device_ids=true, to_apply=%region_14.22 | all-reduce | flops 8192 | bytes 65536 | tf_op jit(solution)/shard_map/psum | solution.py:34
  1011.3 5.8 cholesky.149
  1018.5 4.9 custom-call.35
  1027.7 3.1 copy.250
  1031.5 2.5 gather_fusion.11
  1034.0 6.6 multiply_bitcast_fusion
  1040.6 4.7 copy.194
  1045.2 5.5 fusion.43
  1050.7 6.3 copy.195
  1057.0 5.9 reshape.302
  1063.8 19.7 %all-gather.1 = f32[16,192,64]{1,2,0:T(8,128)S(1)} all-gather(f32[1,192,64]{1,2,0:T(8,128)S(1)} %copy.198), channel_id=1, replica_groups=mesh['sub'=16,'row'=16] {'sub'}, dimensions={0}, use_global_device_ids=true | all-gather | bytes 835584 | tf_op jit(solution)/shard_map/all_gather | solution.py:64
  1091.1 47.1 %all-gather.13.cloned.1.call-done = f32[12288,64]{0,1:T(8,128)} async-done(((f32[768,64]{0,1:T(8,128)}), f32[12288,64]{0,1:T(8,128)}) %all-gather.13.cloned.1.call-update) | async-done | bytes 3145744 | tf_op jit(solution)/shard_map/all_gather | solution.py:45
  1138.2 5.8 copy.237
  1143.9 5.3 gather_fusion.10
  1149.2 6.2 convolution_bitcast_fusion
  1155.4 4.7 copy.190
  1160.1 60.5 %reduce-scatter.17.cloned.1.call-done = f32[768,64]{0,1:T(8,128)} async-done(((f32[12288,64]{0,1:T(8,128)}), f32[768,64]{0,1:T(8,128)}) %reduce-scatter.17.cloned.1.call-update) | async-done | bytes 196624 | tf_op jit(solution)/shard_map/reduce_scatter | solution.py:54
  1222.8 4.3 convolution_add_fusion.3
  1229.7 77.7 %psum.78 = f32[128,64]{0,1:T(8,128)S(1)} all-reduce(f32[128,64]{0,1:T(8,128)S(1)} %fusion.25), channel_id=1, replica_groups=mesh['sub'=16,'row'=16] {'sub','row'}, use_global_device_ids=true, to_apply=%region_18.26 | all-reduce | flops 8192 | bytes 65536 | tf_op jit(solution)/shard_map/psum | solution.py:107
  1307.4 161.1 %all-reduce.7.cloned.1.call-done = f32[128,128]{0,1:T(8,128)} async-done(((f32[128,128]{0,1:T(8,128)}), f32[128,128]{0,1:T(8,128)}) %all-reduce.7.cloned.1.call-update) | async-done | bytes 65552 | tf_op jit(solution)/shard_map/psum | solution.py:107
  1470.3 11.7 cholesky.160
  1483.3 9.8 custom-call.39
  1494.3 74.6 %psum.79 = f32[64,64]{0,1:T(8,128)S(1)} all-reduce(f32[64,64]{0,1:T(8,128)S(1)} %fusion.134), channel_id=1, replica_groups=mesh['sub'=16,'row'=16] {'sub','row'}, use_global_device_ids=true, to_apply=%region_19.27 | all-reduce | flops 4096 | bytes 32768 | tf_op jit(solution)/shard_map/psum | solution.py:115
  1569.0 5.8 cholesky.171
  1576.1 4.9 custom-call.40
  (205 shorter events, 79.0 us)
Async XLA Ops:
  7.2 5.7 copy-start
  7.2 6.1 copy-start.24
  7.2 47.9 %all-gather.9.cloned.1.call-start = ((), (), s32[]{:S(2)}) async-start(), calls=%async_computation.8 | async-start | bytes 1671168 | tf_op jit(solution)/shard_map/all_gather | solution.py:64
  10.1 5.7 copy-start.19
  10.3 5.5 copy-start.1
  11.5 99.6 %reduce-scatter.13.cloned.1.call-start = ((), (), s32[]{:S(2)}) async-start(), calls=%async_computation.9 | async-start | bytes 1671168 | tf_op jit(solution)/shard_map/reduce_scatter | solution.py:71
  12.3 3.6 copy-start.22
  13.2 3.9 copy-start.18
  15.8 1.4 copy-start.2
  15.9 165.8 %all-gather.7.cloned.1.call-start = ((), (), s32[]{:S(2)}) async-start(), calls=%async_computation.6 | async-start | bytes 6684672 | tf_op jit(solution)/shard_map/all_gather | solution.py:45
  16.6 254.2 %reduce-scatter.11.cloned.1.call-start = ((), (), s32[]{:S(2)}) async-start(), calls=%async_computation.7 | async-start | bytes 6684672 | tf_op jit(solution)/shard_map/reduce_scatter | solution.py:54
  17.2 2.5 copy-start.21
  17.2 2.5 copy-start.8
  17.2 5.3 copy-start.16
  37.2 3.6 copy-start.3
  37.3 73.9 %copy-start.29 = (s32[1,1,3]{2,1,0:T(1,128)S(1)}, s32[1,1,3]{2,1,0:T(1,128)}, u32[]{:S(2)}) copy-start(s32[1,1,3]{2,1,0:T(1,128)} %param.28) | copy-start | bytes 40
  37.3 402.2 %reduce-scatter.19.cloned.1.call-start = ((), (), s32[]{:S(2)}) async-start(), calls=%async_computation.16 | async-start | bytes 1671168 | tf_op jit(solution)/shard_map/reduce_scatter | solution.py:71
  40.8 146.0 %copy-start.20 = (s32[1024]{0:T(1024)}, s32[1024]{0:T(1024)S(1)}, u32[]{:S(2)}) copy-start(s32[1024]{0:T(1024)S(1)} %pad_clamp_fusion.4) | copy-start | bytes 12292
  40.9 14.2 copy-start.23
  192.2 83.4 %copy-start.26 = (s32[1,1,12]{2,1,0:T(1,128)S(1)}, s32[1,1,12]{2,1,0:T(1,128)}, u32[]{:S(2)}) copy-start(s32[1,1,12]{2,1,0:T(1,128)} %param.29) | copy-start | bytes 148
  275.6 92.0 %copy-start.17 = (f32[768]{0:T(1024)S(1)}, f32[768]{0:T(1024)}, u32[]{:S(2)}) copy-start(f32[768]{0:T(1024)} %param.24) | copy-start | bytes 9220
  367.6 10.2 copy-start.13
  368.8 9.0 copy-start.4
  377.8 109.3 %all-gather.11.cloned.1.call-start = ((), (), s32[]{:S(2)}) async-start(), calls=%async_computation.10 | async-start | bytes 3342336 | tf_op jit(solution)/shard_map/all_gather | solution.py:45
  378.4 190.8 %reduce-scatter.15.cloned.1.call-start = ((), (), s32[]{:S(2)}) async-start(), calls=%async_computation.11 | async-start | bytes 3342336 | tf_op jit(solution)/shard_map/reduce_scatter | solution.py:54
  410.2 410.0 %all-reduce.5.cloned.1.call-start = ((), (), s32[]{:S(2)}) async-start(), calls=%async_computation.12 | async-start | bytes 131072 | tf_op jit(solution)/shard_map/psum | solution.py:107
  509.0 68.4 %copy-start.27 = (s32[1,1,12]{2,1,0:T(1,128)S(1)}, s32[1,1,12]{2,1,0:T(1,128)}, u32[]{:S(2)}) copy-start(s32[1,1,12]{2,1,0:T(1,128)} %param.29) | copy-start | bytes 148
  573.2 6.0 copy-start.5
  573.2 6.0 copy-start.11
  580.8 508.0 %reduce-scatter.21.cloned.1.call-start = ((), (), s32[]{:S(2)}) async-start(), calls=%async_computation.17 | async-start | bytes 1671168 | tf_op jit(solution)/shard_map/reduce_scatter | solution.py:71
  847.6 178.0 %copy-start.25 = (s32[1,1,12]{2,1,0:T(1,128)S(1)}, s32[1,1,12]{2,1,0:T(1,128)}, u32[]{:S(2)}) copy-start(s32[1,1,12]{2,1,0:T(1,128)} %param.30) | copy-start | bytes 148
  936.4 87.8 %copy-start.9 = (f32[768,64]{0,1:T(8,128)}, f32[768,64]{0,1:T(8,128)S(1)}, u32[]{:S(2)}) copy-start(f32[768,64]{0,1:T(8,128)S(1)} %convolution_bitcast_fusion.13) | copy-start | bytes 589828
  1024.2 6.6 copy-start.6
  1030.8 107.3 %all-gather.13.cloned.1.call-start = ((), (), s32[]{:S(2)}) async-start(), calls=%async_computation.13 | async-start | bytes 3342336 | tf_op jit(solution)/shard_map/all_gather | solution.py:45
  1031.4 189.3 %reduce-scatter.17.cloned.1.call-start = ((), (), s32[]{:S(2)}) async-start(), calls=%async_computation.14 | async-start | bytes 3342336 | tf_op jit(solution)/shard_map/reduce_scatter | solution.py:54
  1063.0 405.5 %all-reduce.7.cloned.1.call-start = ((), (), s32[]{:S(2)}) async-start(), calls=%async_computation.15 | async-start | bytes 131072 | tf_op jit(solution)/shard_map/psum | solution.py:107
  1063.8 24.2 %copy-start.14 = (f32[768,64]{0,1:T(8,128)S(1)}, f32[768,64]{0,1:T(8,128)}, u32[]{:S(2)}) copy-start(f32[768,64]{0,1:T(8,128)} %fusion.42) | copy-start | bytes 589828
  1083.5 4.9 copy-start.15
  1083.5 5.4 copy-start.30
  1160.1 67.0 %copy-start.12 = (f32[12,64,64]{2,0,1:T(8,128)S(1)}, f32[12,64,64]{2,0,1:T(8,128)}, u32[]{:S(2)}) copy-start(f32[12,64,64]{2,0,1:T(8,128)} %fusion.36) | copy-start | bytes 589828
  1160.1 67.0 %copy-start.28 = (s32[1,1,12]{2,1,0:T(1,128)S(1)}, s32[1,1,12]{2,1,0:T(1,128)}, u32[]{:S(2)}) copy-start(s32[1,1,12]{2,1,0:T(1,128)} %param.29) | copy-start | bytes 148
  1222.8 5.2 copy-start.7
  1227.1 2.0 copy-start.10
Sparse Core Ops, SparseCore 0:
  11.7 43.3 all-gather.8
  57.6 53.5 reduce-scatter.12
  113.9 67.7 all-gather.6
  185.7 85.0 reduce-scatter.10
  377.9 52.2 reduce-scatter.18
  433.1 53.9 all-gather.10
  490.7 78.4 reduce-scatter.14
  580.9 239.1 all-reduce.4
  1030.9 50.4 reduce-scatter.20
  1084.0 54.0 all-gather.12
  1142.2 78.3 reduce-scatter.16
  1229.3 239.1 all-reduce.6
where the time goes:
time: 1590 us
  waiting for transfers between devices  751 us (47%)
  blocking collectives  497 us (31%)
  local copies, waits for them, and re-layouts  128 us (8%)
  matrix products  100 us (6%)
  other arithmetic  97.2 us (6%)
    psum x2, waiting for transfers between devices, local(): lax.psum((gram_product(basis, image_b), gram_product(basis, image_x)), ('...  321 us
    reduce_scatter x6, waiting for transfers between devices, apply_blocks(): lax.psum_scatter(jnp.einsum('bk,kiw->biw', chosen, backward, precision=pr...  253 us
    all_gather x3, waiting for transfers between devices, apply_blocks(): lax.all_gather(vector, 'row', axis=0, tiled=True).reshape(-1, KB, width)  162 us
    psum x2, blocking collectives, local(): lax.psum((gram_product(basis, image_b), gram_product(basis, image_x)), ('...  156 us
    psum x2, blocking collectives, project(): lax.psum((gram_product(current, current), gram_product(current, image_x))...  151 us
    psum x2, blocking collectives, local(): lengths = lax.psum(gram_product(moved, moved), ('sub', 'row'))  149 us
    all_gather x2, blocking collectives, apply_blocks(): lax.all_gather(boundary, 'sub', axis=0, tiled=True).reshape(-1, KB, width)  41.6 us
    another operation x12, other arithmetic, chol_solve(): factor = jnp.linalg.cholesky(matrix)  37.8 us
  transfers between devices with their start and end apart: 12, of which 10 were waited for; matrix products, arithmetic and copies ran while one was open for 11% of the time, Pallas kernels for 0%

commit v1 on v0

--- a/solution.py
+++ b/solution.py
@@ -112,7 +112,7 @@
         step_a = full_dot(image_b, coeffs)
         moved = current + step_x
         moved_image = image_x + step_a
-        lengths = lax.psum(gram_product(moved, moved), ("sub", "row"))
+        lengths = jnp.sum(lax.all_gather(gram_product(moved, moved), ("sub", "row")), axis=0)
         factor = jnp.linalg.cholesky(lengths / total_rows)
         current = rescale(factor, moved)
         image_x = rescale(factor, moved_image)

time: 1590 us -> 1680 us (1.057)
  waiting for transfers between devices: 751 us -> 981 us
  blocking collectives: 497 us -> 349 us
    all_gather x0 -> x2, waiting for transfers between devices: none -> 229 us  [local(): lax.all_gather(gram_product(moved, moved), ('sub', 'row'))]
    psum x2 -> x0, blocking collectives: 149 us -> none  [local(): lengths = lax.psum(gram_product(moved, moved), ('sub', 'row'))]
  transfers between devices with their start and end apart: 12 -> 14, of which waited for: 10 -> 12; matrix products, arithmetic and copies ran while one was open for 11% -> 10% of each run, Pallas kernels for 0% -> 0%
where the time goes in v1:
time: 1680 us
  waiting for transfers between devices  981 us (58%)
  blocking collectives  349 us (21%)
  local copies, waits for them, and re-layouts  128 us (8%)
  other arithmetic  105 us (6%)
  matrix products  99.4 us (6%)
    psum x2, waiting for transfers between devices, local(): lax.psum((gram_product(basis, image_b), gram_product(basis, image_x)), ('...  321 us
    reduce_scatter x6, waiting for transfers between devices, apply_blocks(): lax.psum_scatter(jnp.einsum('bk,kiw->biw', chosen, backward, precision=pr...  253 us
    all_gather x2, waiting for transfers between devices, local(): lax.all_gather(gram_product(moved, moved), ('sub', 'row'))  229 us
    all_gather x3, waiting for transfers between devices, apply_blocks(): lax.all_gather(vector, 'row', axis=0, tiled=True).reshape(-1, KB, width)  162 us
    psum x2, blocking collectives, local(): lax.psum((gram_product(basis, image_b), gram_product(basis, image_x)), ('...  156 us
    psum x2, blocking collectives, project(): lax.psum((gram_product(current, current), gram_product(current, image_x))...  152 us
    all_gather x2, blocking collectives, apply_blocks(): lax.all_gather(boundary, 'sub', axis=0, tiled=True).reshape(-1, KB, width)  41.7 us
    another operation x12, other arithmetic, chol_solve(): factor = jnp.linalg.cholesky(matrix)  37.8 us
  transfers between devices with their start and end apart: 14, of which 12 were waited for; matrix products, arithmetic and copies ran while one was open for 10% of the time, Pallas kernels for 0%

profile of v1, /device:TPU:1, one launch (start us, length us, event | category | flops | bytes accessed | tf_op | source)
XLA Modules:
  0.0 1679.4 jit_solution(10720067873756686466)
XLA Ops:
  19.7 2.8 copy.138
  22.6 3.7 multiply_bitcast_fusion.2
  26.3 4.6 fusion
  31.0 6.3 copy.140
  37.5 3.3 copy.136
  41.8 13.2 all-gather.13.cloned.1.call-done
  57.4 53.8 %reduce-scatter.13.cloned.1.call-done = f32[192,128]{1,0:T(8,128)} async-done(((f32[3072,128]{1,0:T(8,128)}), f32[192,128]{1,0:T(8,128)}) %reduce-scatter.13.cloned.1.call-update) | async-done | bytes 98320 | tf_op jit(solution)/shard_map/reduce_scatter | solution.py:71
  112.6 69.1 %all-gather.11.cloned.1.call-done = f32[12288,128]{1,0:T(8,128)} async-done(((f32[768,128]{1,0:T(8,128)}), f32[12288,128]{1,0:T(8,128)}) %all-gather.11.cloned.1.call-update) | async-done | bytes 6291472 | tf_op jit(solution)/shard_map/all_gather | solution.py:45
  181.7 5.2 gather_fusion
  186.9 5.3 convolution_bitcast_fusion.2
  192.2 78.6 %reduce-scatter.11.cloned.1.call-done = f32[768,128]{1,0:T(8,128)} async-done(((f32[12288,128]{1,0:T(8,128)}), f32[768,128]{1,0:T(8,128)}) %reduce-scatter.11.cloned.1.call-update) | async-done | bytes 393232 | tf_op jit(solution)/shard_map/reduce_scatter | solution.py:54
  270.8 4.8 fusion.7
  277.3 76.9 %all-reduce.1 = (f32[64,64]{0,1:T(8,128)S(1)}, f32[64,64]{0,1:T(8,128)S(1)}) all-reduce(f32[64,64]{0,1:T(8,128)S(1)} %convolution_bitcast_fusion.16, f32[64,64]{0,1:T(8,128)} %fusion.130), channel_id=1, replica_groups=mesh['sub'=16,'row'=16] {'sub','row'}, use_global_device_ids=true, to_apply=%region_5.0 | all-reduce | flops 8192 | bytes 65536 | tf_op jit(solution)/shard_map/psum | solution.py:34
  354.3 5.8 cholesky.116
  361.5 4.9 custom-call.29
  371.9 2.8 fusion.15
  374.7 3.1 copy.238
  381.2 6.5 multiply_bitcast_fusion.1
  387.7 4.7 copy.158
  392.4 5.4 fusion.44
  397.9 6.3 copy.159
  404.2 5.9 reshape.293
  410.9 21.9 %all-gather.2 = f32[16,192,64]{1,2,0:T(8,128)} all-gather(f32[1,192,64]{1,2,0:T(8,128)S(1)} %copy.162), channel_id=1, replica_groups=mesh['sub'=16,'row'=16] {'sub'}, dimensions={0}, use_global_device_ids=true | all-gather | bytes 835584 | tf_op jit(solution)/shard_map/all_gather | solution.py:64
  432.8 2.9 copy.226
  441.6 45.5 %all-gather.15.cloned.1.call-done = f32[12288,64]{0,1:T(8,128)} async-done(((f32[768,64]{0,1:T(8,128)}), f32[12288,64]{0,1:T(8,128)}) %all-gather.15.cloned.1.call-update) | async-done | bytes 3145744 | tf_op jit(solution)/shard_map/all_gather | solution.py:45
  487.1 5.7 copy.225
  492.8 5.3 gather_fusion.5
  498.1 6.2 convolution_bitcast_fusion.1
  504.3 4.7 copy.154
  509.0 60.2 %reduce-scatter.15.cloned.1.call-done = f32[768,64]{0,1:T(8,128)} async-done(((f32[12288,64]{0,1:T(8,128)}), f32[768,64]{0,1:T(8,128)}) %reduce-scatter.15.cloned.1.call-update) | async-done | bytes 196624 | tf_op jit(solution)/shard_map/reduce_scatter | solution.py:54
  573.2 4.3 convolution_add_fusion.4
  582.2 77.9 %psum.59 = f32[128,64]{0,1:T(8,128)S(1)} all-reduce(f32[128,64]{0,1:T(8,128)} %fusion.27), channel_id=1, replica_groups=mesh['sub'=16,'row'=16] {'sub','row'}, use_global_device_ids=true, to_apply=%region_11.16 | all-reduce | flops 8192 | bytes 65536 | tf_op jit(solution)/shard_map/psum | solution.py:107
  660.2 160.0 %all-reduce.5.cloned.1.call-done = f32[128,128]{0,1:T(8,128)} async-done(((f32[128,128]{0,1:T(8,128)}), f32[128,128]{0,1:T(8,128)}) %all-reduce.5.cloned.1.call-update) | async-done | bytes 65552 | tf_op jit(solution)/shard_map/psum | solution.py:107
  822.0 11.7 cholesky.127
  835.0 9.8 custom-call.31
  847.9 114.3 %all-gather.19.cloned.1.call-done = f32[16384,64]{1,0:T(8,128)} async-done(((f32[64,64]{1,0:T(8,128)}), f32[16384,64]{1,0:T(8,128)}) %all-gather.19.cloned.1.call-update) | async-done | bytes 4194320 | tf_op jit(solution)/shard_map/all_gather | solution.py:115
  962.2 4.0 reduce_sum.18
  966.4 5.8 cholesky.138
  973.5 4.9 custom-call.32
  979.8 75.0 %all-reduce = (f32[64,64]{1,0:T(8,128)S(1)}, f32[64,64]{0,1:T(8,128)S(1)}) all-reduce(f32[64,64]{1,0:T(8,128)S(1)} %fusion.133, f32[64,64]{0,1:T(8,128)S(1)} %fusion.132), channel_id=1, replica_groups=mesh['sub'=16,'row'=16] {'sub','row'}, use_global_device_ids=true, to_apply=%region_14.22 | all-reduce | flops 8192 | bytes 65536 | tf_op jit(solution)/shard_map/psum | solution.py:34
  1054.9 5.8 cholesky.149
  1061.9 4.9 custom-call.35
  1071.1 3.1 copy.242
  1077.6 6.5 multiply_bitcast_fusion
  1084.1 4.7 copy.188
  1088.8 5.5 fusion.43
  1094.3 6.3 copy.189
  1100.6 5.9 reshape.302
  1107.4 19.9 %all-gather.3 = f32[16,192,64]{1,2,0:T(8,128)S(1)} all-gather(f32[1,192,64]{1,2,0:T(8,128)S(1)} %copy.192), channel_id=1, replica_groups=mesh['sub'=16,'row'=16] {'sub'}, dimensions={0}, use_global_device_ids=true | all-gather | bytes 835584 | tf_op jit(solution)/shard_map/all_gather | solution.py:64
  1134.8 47.9 %all-gather.17.cloned.1.call-done = f32[12288,64]{0,1:T(8,128)} async-done(((f32[768,64]{0,1:T(8,128)}), f32[12288,64]{0,1:T(8,128)}) %all-gather.17.cloned.1.call-update) | async-done | bytes 3145744 | tf_op jit(solution)/shard_map/all_gather | solution.py:45
  1182.7 5.7 copy.229
  1188.4 5.3 gather_fusion.10
  1193.7 6.2 convolution_bitcast_fusion
  1199.9 4.7 copy.184
  1204.6 60.5 %reduce-scatter.17.cloned.1.call-done = f32[768,64]{0,1:T(8,128)} async-done(((f32[12288,64]{0,1:T(8,128)}), f32[768,64]{0,1:T(8,128)}) %reduce-scatter.17.cloned.1.call-update) | async-done | bytes 196624 | tf_op jit(solution)/shard_map/reduce_scatter | solution.py:54
  1267.3 4.3 convolution_add_fusion.3
  1274.2 77.7 %psum.63 = f32[128,64]{0,1:T(8,128)S(1)} all-reduce(f32[128,64]{0,1:T(8,128)S(1)} %fusion.25), channel_id=1, replica_groups=mesh['sub'=16,'row'=16] {'sub','row'}, use_global_device_ids=true, to_apply=%region_18.26 | all-reduce | flops 8192 | bytes 65536 | tf_op jit(solution)/shard_map/psum | solution.py:107
  1351.9 161.1 %all-reduce.7.cloned.1.call-done = f32[128,128]{0,1:T(8,128)} async-done(((f32[128,128]{0,1:T(8,128)}), f32[128,128]{0,1:T(8,128)}) %all-reduce.7.cloned.1.call-update) | async-done | bytes 65552 | tf_op jit(solution)/shard_map/psum | solution.py:107
  1514.8 11.7 cholesky.160
  1527.8 9.8 custom-call.39
  1539.4 114.9 %all-gather.21.cloned.1.call-done = f32[16384,64]{1,0:T(8,128)} async-done(((f32[64,64]{1,0:T(8,128)}), f32[16384,64]{1,0:T(8,128)}) %all-gather.21.cloned.1.call-update) | async-done | bytes 4194320 | tf_op jit(solution)/shard_map/all_gather | solution.py:115
  1654.3 4.0 reduce_sum.19
  1658.5 5.8 cholesky.171
  1665.7 4.9 custom-call.40
  (217 shorter events, 84.0 us)
Async XLA Ops:
  7.2 5.7 copy-start
  7.2 6.1 copy-start.26
  7.2 47.9 %all-gather.13.cloned.1.call-start = ((), (), s32[]{:S(2)}) async-start(), calls=%async_computation.8 | async-start | bytes 1671168 | tf_op jit(solution)/shard_map/all_gather | solution.py:64
  10.1 5.7 copy-start.21
  10.3 5.5 copy-start.1
  11.5 99.6 %reduce-scatter.13.cloned.1.call-start = ((), (), s32[]{:S(2)}) async-start(), calls=%async_computation.9 | async-start | bytes 1671168 | tf_op jit(solution)/shard_map/reduce_scatter | solution.py:71
  12.3 3.6 copy-start.24
  13.2 3.9 copy-start.20
  15.8 1.4 copy-start.2
  15.9 165.8 %all-gather.11.cloned.1.call-start = ((), (), s32[]{:S(2)}) async-start(), calls=%async_computation.6 | async-start | bytes 6684672 | tf_op jit(solution)/shard_map/all_gather | solution.py:45
  16.6 254.2 %reduce-scatter.11.cloned.1.call-start = ((), (), s32[]{:S(2)}) async-start(), calls=%async_computation.7 | async-start | bytes 6684672 | tf_op jit(solution)/shard_map/reduce_scatter | solution.py:54
  17.2 2.5 copy-start.23
  17.2 2.5 copy-start.8
  17.3 5.3 copy-start.18
  37.3 3.6 copy-start.3
  37.3 73.9 %copy-start.31 = (s32[1,1,3]{2,1,0:T(1,128)S(1)}, s32[1,1,3]{2,1,0:T(1,128)}, u32[]{:S(2)}) copy-start(s32[1,1,3]{2,1,0:T(1,128)} %param.28) | copy-start | bytes 40
  37.3 402.1 %reduce-scatter.19.cloned.1.call-start = ((), (), s32[]{:S(2)}) async-start(), calls=%async_computation.18 | async-start | bytes 1671168 | tf_op jit(solution)/shard_map/reduce_scatter | solution.py:71
  40.9 146.0 %copy-start.22 = (s32[1024]{0:T(1024)}, s32[1024]{0:T(1024)S(1)}, u32[]{:S(2)}) copy-start(s32[1024]{0:T(1024)S(1)} %pad_clamp_fusion.4) | copy-start | bytes 12292
  40.9 14.2 copy-start.25
  192.2 83.4 %copy-start.28 = (s32[1,1,12]{2,1,0:T(1,128)S(1)}, s32[1,1,12]{2,1,0:T(1,128)}, u32[]{:S(2)}) copy-start(s32[1,1,12]{2,1,0:T(1,128)} %param.29) | copy-start | bytes 148
  275.6 92.0 %copy-start.19 = (f32[768]{0:T(1024)S(1)}, f32[768]{0:T(1024)}, u32[]{:S(2)}) copy-start(f32[768]{0:T(1024)} %param.24) | copy-start | bytes 9220
  367.6 10.2 copy-start.13
  368.8 9.0 copy-start.4
  377.8 109.3 %all-gather.15.cloned.1.call-start = ((), (), s32[]{:S(2)}) async-start(), calls=%async_computation.10 | async-start | bytes 3342336 | tf_op jit(solution)/shard_map/all_gather | solution.py:45
  378.4 190.8 %reduce-scatter.15.cloned.1.call-start = ((), (), s32[]{:S(2)}) async-start(), calls=%async_computation.11 | async-start | bytes 3342336 | tf_op jit(solution)/shard_map/reduce_scatter | solution.py:54
  410.1 410.0 %all-reduce.5.cloned.1.call-start = ((), (), s32[]{:S(2)}) async-start(), calls=%async_computation.12 | async-start | bytes 131072 | tf_op jit(solution)/shard_map/psum | solution.py:107
  509.0 68.4 %copy-start.29 = (s32[1,1,12]{2,1,0:T(1,128)S(1)}, s32[1,1,12]{2,1,0:T(1,128)}, u32[]{:S(2)}) copy-start(s32[1,1,12]{2,1,0:T(1,128)} %param.29) | copy-start | bytes 148
  573.2 6.0 copy-start.5
  573.2 6.0 copy-start.11
  580.8 381.4 %all-gather.19.cloned.1.call-start = ((), (), s32[]{:S(2)}) async-start(), calls=%async_computation.16 | async-start | bytes 8421376 | tf_op jit(solution)/shard_map/all_gather | solution.py:115
  847.3 285.4 %reduce-scatter.21.cloned.1.call-start = ((), (), s32[]{:S(2)}) async-start(), calls=%async_computation.19 | async-start | bytes 1671168 | tf_op jit(solution)/shard_map/reduce_scatter | solution.py:71
  847.9 130.9 %copy-start.15 = (f32[768,64]{0,1:T(8,128)}, f32[768,64]{0,1:T(8,128)S(1)}, u32[]{:S(2)}) copy-start(f32[768,64]{0,1:T(8,128)S(1)} %fusion.42) | copy-start | bytes 589828
  962.2 16.6 copy-start.14
  966.2 102.8 %copy-start.27 = (s32[1,1,12]{2,1,0:T(1,128)S(1)}, s32[1,1,12]{2,1,0:T(1,128)}, u32[]{:S(2)}) copy-start(s32[1,1,12]{2,1,0:T(1,128)} %param.30) | copy-start | bytes 148
  979.2 88.5 %copy-start.9 = (f32[768,64]{0,1:T(8,128)}, f32[768,64]{0,1:T(8,128)S(1)}, u32[]{:S(2)}) copy-start(f32[768,64]{0,1:T(8,128)S(1)} %convolution_bitcast_fusion.13) | copy-start | bytes 589828
  1067.6 6.6 copy-start.6
  1074.3 108.4 %all-gather.17.cloned.1.call-start = ((), (), s32[]{:S(2)}) async-start(), calls=%async_computation.13 | async-start | bytes 3342336 | tf_op jit(solution)/shard_map/all_gather | solution.py:45
  1075.0 190.1 %reduce-scatter.17.cloned.1.call-start = ((), (), s32[]{:S(2)}) async-start(), calls=%async_computation.14 | async-start | bytes 3342336 | tf_op jit(solution)/shard_map/reduce_scatter | solution.py:54
  1106.5 406.4 %all-reduce.7.cloned.1.call-start = ((), (), s32[]{:S(2)}) async-start(), calls=%async_computation.15 | async-start | bytes 131072 | tf_op jit(solution)/shard_map/psum | solution.py:107
  1107.4 24.4 %copy-start.16 = (f32[768,64]{0,1:T(8,128)S(1)}, f32[768,64]{0,1:T(8,128)}, u32[]{:S(2)}) copy-start(f32[768,64]{0,1:T(8,128)} %copy-done.15) | copy-start | bytes 589828
  1127.2 5.0 copy-start.17
  1127.3 5.4 copy-start.32
  1204.6 66.9 %copy-start.12 = (f32[12,64,64]{2,0,1:T(8,128)S(1)}, f32[12,64,64]{2,0,1:T(8,128)}, u32[]{:S(2)}) copy-start(f32[12,64,64]{2,0,1:T(8,128)} %fusion.36) | copy-start | bytes 589828
  1204.6 66.9 %copy-start.30 = (s32[1,1,12]{2,1,0:T(1,128)S(1)}, s32[1,1,12]{2,1,0:T(1,128)}, u32[]{:S(2)}) copy-start(s32[1,1,12]{2,1,0:T(1,128)} %param.29) | copy-start | bytes 148
  1267.3 5.2 copy-start.7
  1271.5 2.1 copy-start.10
  1273.6 380.7 %all-gather.21.cloned.1.call-start = ((), (), s32[]{:S(2)}) async-start(), calls=%async_computation.17 | async-start | bytes 8421376 | tf_op jit(solution)/shard_map/all_gather | solution.py:115
Sparse Core Ops, SparseCore 0:
  11.7 43.3 all-gather.12
  57.6 53.5 reduce-scatter.12
  113.9 67.7 all-gather.10
  185.7 85.0 reduce-scatter.10
  378.0 52.3 reduce-scatter.18
  433.2 53.8 all-gather.14
  490.7 78.4 reduce-scatter.14
  580.9 239.1 all-reduce.4
  847.4 114.7 all-gather.18
  1074.4 51.4 reduce-scatter.20
  1128.6 54.0 all-gather.16
  1186.6 78.4 reduce-scatter.16
  1273.7 239.1 all-reduce.6
  1539.5 114.7 all-gather.20
